TPU v7x, 128 devices: a whole 4x4x4 slice. The times are simulated.
128 devices in a mesh: row: 16 (over z_lo, x, core), col: 8 (over y, z_hi).
Axes of the slice: x: 4, y: 4, z: 4 (z_hi: 2, z_lo: 2; z = z_hi * 2 + z_lo), core: 2. Of those that a mesh axis runs over, the one named last changes fastest.
Arguments:
- grad: float32 [5120, 8192], P('row', 'col'), may hold values from -180 to 180
- momentum: float32 [5120, 8192], P('row', 'col'), may hold values from -30 to 30
Outputs:
- update: bfloat16 [5120, 8192], P('row', 'col')
- new_momentum: float32 [5120, 8192], P('row', 'col')
All inputs are finite; a program needn't handle non-finite values.
Results may differ from a plain program's by a relative error of at most 0.0013.
The roundings to bfloat16 on the way count: a program that leaves them out, or rounds other values in their place, can miss the bound.
Values may be sent and summed in bfloat16 or wider, within the bound.
A program may use at most 128 MiB of HBM per device.

v0:
```python
import math

import jax
import jax.numpy as jnp
from jax import lax
from jax.sharding import PartitionSpec as P

momentum_decay = 0.95
target_rms = 0.25
norm_epsilon = 1e-07
coef_linear = 3.4445
coef_cubic = -4.775
coef_quintic = 2.0315


def from_root(value, axis, source):
    kept = jnp.where(lax.axis_index(axis) == source, value, 0).astype(value.dtype)
    return lax.psum(kept, axis)


def per_device(grad, momentum):
    tile_rows, tile_cols = grad.shape
    row_devices = lax.axis_size("row")
    col_devices = lax.axis_size("col")
    row_ratio = row_devices // col_devices
    total_rows = tile_rows * row_devices
    total_cols = tile_cols * col_devices
    new_momentum = momentum_decay * momentum + grad
    blended = (grad + momentum_decay * new_momentum).astype(jnp.bfloat16)
    column = lax.all_gather(blended, "row", axis=0, tiled=True)
    tile_wide = blended.astype(jnp.float32)
    squares_total = lax.psum(jnp.sum(tile_wide * tile_wide), ("row", "col"))
    norm_scale = target_rms * math.sqrt(total_rows) / (jnp.sqrt(squares_total) + norm_epsilon)
    ortho_column = (column.astype(jnp.float32) * norm_scale).astype(jnp.bfloat16)
    ortho_tile = lax.dynamic_slice_in_dim(
        ortho_column, lax.axis_index("row") * tile_rows, tile_rows, 0
    )
    gram_mirror = lax.psum_scatter(
        lax.dot_general(
            ortho_column, ortho_tile, (((1,), (1,)), ((), ())), preferred_element_type=jnp.float32
        ),
        "col",
        scatter_dimension=0,
        tiled=True,
    )
    gram_tile = gram_mirror.T.astype(jnp.bfloat16)
    gram_rows = lax.all_gather(gram_tile, "col", axis=1, tiled=True)
    strips = []
    for offset in range(row_ratio):
        root_index = lax.axis_index("col") * row_ratio + offset
        strips.append(from_root(gram_rows, "row", root_index))
    partner = jnp.concatenate(strips, axis=0)
    square = lax.dot_general(
        gram_rows, partner, (((1,), (1,)), ((), ())), preferred_element_type=jnp.float32
    )
    poly_tile = (coef_cubic * gram_tile.astype(jnp.float32) + coef_quintic * square).astype(
        jnp.bfloat16
    )
    poly_rows = lax.all_gather(poly_tile, "col", axis=1, tiled=True)
    product = jnp.dot(poly_rows, ortho_column, preferred_element_type=jnp.float32)
    update = (
        math.sqrt(total_cols) * (coef_linear * ortho_tile.astype(jnp.float32) + product)
    ).astype(jnp.bfloat16)
    return (update, new_momentum)


def solution(mesh):
    placed = (P("row", "col"), P("row", "col"))
    return jax.shard_map(
        per_device,
        mesh=mesh,
        in_specs=placed,
        out_specs=(P("row", "col"), P("row", "col")),
        check_vma=False,
    )
```

profile of v0, /device:TPU:1, one launch (start us, length us, event | category | flops | bytes accessed | tf_op | source)
XLA Modules:
  0.0 494.7 jit_solution(6061522356071396134)
XLA Ops:
  7.2 0.0 all-gather.4.cloned.1.call-start
  7.2 4.1 multiply_reduce_fusion
  11.3 0.0 all-gather.4.cloned.1.call-update
  11.3 0.0 reduce-scatter.2.cloned.1.call-start
  11.4 68.7 %psum.21 = f32[]{:T(128)} all-reduce(f32[]{:T(128)} %get-tuple-element.4), channel_id=1, replica_groups=mesh['row'=16,'col'=8] {'row','col'}, use_global_device_ids=true, to_apply=%region_1.0 | all-reduce | flops 1 | bytes 8 | tf_op jit(solution)/shard_map/psum | solution.py:32
  80.8 0.0 all-gather.4.cloned.1.call-done
  80.9 11.1 %multiply_convert_fusion = bf16[5120,1024]{1,0:T(8,128)(2,1)} fusion(bf16[5120,1024]{1,0:T(8,128)(2,1)} %all-gather.4.cloned.1.call-done, f32[]{:T(128)S(6)} %div.3), kind=kLoop, calls=%fused_computation | loop fusion | flops 15728640 | bytes 20971524 | tf_op jit(solution)/shard_map/convert_element_type | solution.py:34
  92.0 10.3 %fusion.15 = f32[5120,320]{0,1:T(8,128)} fusion(bf16[5120,1024]{1,0:T(8,128)(2,1)} %multiply_convert_fusion, s32[]{:T(128)S(6)} %select_n.17), kind=kOutput, calls=%fused_computation.16 | convolution fusion | flops 3355443200 | bytes 17694724 | tf_op jit(solution)/shard_map/dot_general | solution.py:39
  102.3 0.0 reduce-scatter.2.cloned.1.call-update
  102.4 0.0 all-gather.6.cloned.1.call-start
  102.4 99.3 %reduce-scatter.2.cloned.1.call-done = f32[640,320]{0,1:T(8,128)} async-done(((f32[5120,320]{0,1:T(8,128)}), f32[640,320]{0,1:T(8,128)}) %reduce-scatter.2.cloned.1.call-update) | async-done | bytes 819216 | tf_op jit(solution)/shard_map/reduce_scatter | solution.py:38
  201.7 1.9 convert_bitcast_fusion
  203.6 0.0 all-gather.6.cloned.1.call-update
  203.7 0.0 all-reduce.3.cloned.1.call-start
  203.7 63.5 %all-gather.6.cloned.1.call-done = bf16[320,5120]{1,0:T(8,128)(2,1)} async-done(((bf16[320,640]{1,0:T(8,128)(2,1)}), bf16[320,5120]{1,0:T(8,128)(2,1)}) %all-gather.6.cloned.1.call-update) | async-done | bytes 3276816 | tf_op jit(solution)/shard_map/all_gather | solution.py:47
  267.3 5.1 %broadcast_select_fusion.1 = (bf16[320,5120]{1,0:T(8,128)(2,1)}, bf16[320,5120]{1,0:T(8,128)(2,1)}) fusion(bf16[320,5120]{1,0:T(8,128)(2,1)} %all-gather.6.cloned.1.call-done, pred[]{:T(512)S(6)} %eq.6, pred[]{:T(512)S(6)} %eq.7), kind=kLoop, calls=%fused_computation.6 | loop fusion | flops 3276800 | bytes 9830402 | tf_op jit(solution)/shard_map/jit(_where)/select_n | solution.py:17
  272.4 0.0 copy-start
  272.4 0.0 all-reduce.3.cloned.1.call-update
  272.4 0.2 all-gather.8.cloned.1.call-start
  272.6 134.4 %all-reduce.3.cloned.1.call-done = (bf16[320,5120]{1,0:T(8,128)(2,1)}, bf16[320,5120]{1,0:T(8,128)(2,1)}) async-done(((bf16[320,5120]{1,0:T(8,128)(2,1)}, bf16[320,5120]{1,0:T(8,128)(2,1)}), (bf16[320,5120]{1,0:T(8,128)(2,1)}, bf16[320,5120]{1,0:T(8,128)(2,1)})) %all-reduce.3.cloned.1.call-update) | async-done | bytes 6553616 | tf_op jit(solution)/shard_map/psum | solution.py:18
  407.0 0.0 copy-done
  407.0 6.4 %fusion.12 = bf16[320,640]{1,0:T(8,128)(2,1)} fusion(bf16[320,5120]{1,0:T(8,128)(2,1)S(1)} %copy-done, bf16[320,5120]{1,0:T(8,128)(2,1)} %get-tuple-element.2, bf16[320,5120]{1,0:T(8,128)(2,1)} %get-tuple-element.3, bf16[320,640]{1,0:T(8,128)(2,1)} %convert_bitcast_fusion), kind=kOutput, calls=%fused_computation.15 | convolution fusion | flops 2111283200 | bytes 10649600 | tf_op jit(solution)/shard_map/dot_general | solution.py:53
  413.4 0.0 all-gather.8.cloned.1.call-update
  413.4 65.3 %all-gather.8.cloned.1.call-done = bf16[320,5120]{1,0:T(8,128)(2,1)} async-done(((bf16[320,640]{1,0:T(8,128)(2,1)}), bf16[320,5120]{1,0:T(8,128)(2,1)}) %all-gather.8.cloned.1.call-update) | async-done | bytes 3276816 | tf_op jit(solution)/shard_map/all_gather | solution.py:59
  478.8 9.4 %fusion.5 = bf16[320,1024]{1,0:T(8,128)(2,1)} fusion(bf16[320,5120]{1,0:T(8,128)(2,1)} %all-gather.8.cloned.1.call-done, bf16[5120,1024]{1,0:T(8,128)(2,1)} %multiply_convert_fusion, s32[]{:T(128)S(6)} %select_n.17), kind=kOutput, calls=%fused_computation.9 | convolution fusion | flops 3357081600 | bytes 15073284 | tf_op jit(solution)/shard_map/dot_general | solution.py:60
Async XLA Ops:
  7.2 73.7 %all-gather.4.cloned.1.call-start = ((), (), s32[]{:S(2)}) async-start(), calls=%async_computation.1 | async-start | bytes 11141120 | tf_op jit(solution)/shard_map/all_gather | solution.py:30
  11.3 190.4 %reduce-scatter.2.cloned.1.call-start = ((), (), s32[]{:S(2)}) async-start(), calls=%async_computation.2 | async-start | bytes 7372800 | tf_op jit(solution)/shard_map/reduce_scatter | solution.py:38
  102.4 164.9 %all-gather.6.cloned.1.call-start = ((), (), s32[]{:S(2)}) async-start(), calls=%async_computation.3 | async-start | bytes 3686400 | tf_op jit(solution)/shard_map/all_gather | solution.py:47
  203.7 203.3 %all-reduce.3.cloned.1.call-start = ((), (), s32[]{:S(2)}) async-start(), calls=%async_computation.5 | async-start | bytes 13107200 | tf_op jit(solution)/shard_map/psum | solution.py:18
  272.4 134.6 %copy-start = (bf16[320,5120]{1,0:T(8,128)(2,1)S(1)}, bf16[320,5120]{1,0:T(8,128)(2,1)}, u32[]{:S(2)}) copy-start(bf16[320,5120]{1,0:T(8,128)(2,1)} %all-gather.6.cloned.1.call-done) | copy-start | bytes 9830404
  272.4 206.4 %all-gather.8.cloned.1.call-start = ((), (), s32[]{:S(2)}) async-start(), calls=%async_computation.4 | async-start | bytes 3686400 | tf_op jit(solution)/shard_map/all_gather | solution.py:59
Sparse Core Ops, SparseCore 0:
  11.5 66.8 all-gather.3
  102.5 99.1 reduce-scatter.1
  204.9 62.3 all-gather.5
  272.5 134.4 all-reduce.2
  413.6 65.1 all-gather.7
where the time goes:
time: 495 us
  waiting for transfers between devices  363 us (73%)
  blocking collectives  68.7 us (14%)
  matrix products  26.2 us (5%)
  other arithmetic  22.3 us (5%)
  between operations  14.5 us (3%)
    psum x1, waiting for transfers between devices, from_root(): return lax.psum(kept, axis)  134 us
    reduce_scatter x1, waiting for transfers between devices, per_device(): lax.psum_scatter(lax.dot_general(ortho_column, ortho_tile, (((1,), (1,)),...  99.3 us
    psum x1, blocking collectives, per_device(): squares_total = lax.psum(jnp.sum(tile_wide * tile_wide), ('row', 'col'))  68.7 us
    all_gather x1, waiting for transfers between devices, per_device(): poly_rows = lax.all_gather(poly_tile, 'col', axis=1, tiled=True)  65.3 us
    all_gather x1, waiting for transfers between devices, per_device(): gram_rows = lax.all_gather(gram_tile, 'col', axis=1, tiled=True)  63.5 us
    convert_element_type x1, other arithmetic, per_device(): (column.astype(jnp.float32) * norm_scale).astype(jnp.bfloat16)  11.1 us
    dot_general x1, matrix products, per_device(): lax.dot_general(ortho_column, ortho_tile, (((1,), (1,)), ((), ())), prefe...  10.3 us
  transfers between devices with their start and end apart: 5, of which 4 were waited for; matrix products, arithmetic and copies ran while one was open for 0% of the time, Pallas kernels for 0%

commit v1 on v0

--- a/solution.py
+++ b/solution.py
@@ -13,16 +13,10 @@
 coef_quintic = 2.0315
 
 
-def from_root(value, axis, source):
-    kept = jnp.where(lax.axis_index(axis) == source, value, 0).astype(value.dtype)
-    return lax.psum(kept, axis)
-
-
 def per_device(grad, momentum):
     tile_rows, tile_cols = grad.shape
     row_devices = lax.axis_size("row")
     col_devices = lax.axis_size("col")
-    row_ratio = row_devices // col_devices
     total_rows = tile_rows * row_devices
     total_cols = tile_cols * col_devices
     new_momentum = momentum_decay * momentum + grad
@@ -45,14 +39,8 @@
     )
     gram_tile = gram_mirror.T.astype(jnp.bfloat16)
     gram_rows = lax.all_gather(gram_tile, "col", axis=1, tiled=True)
-    strips = []
-    for offset in range(row_ratio):
-        root_index = lax.axis_index("col") * row_ratio + offset
-        strips.append(from_root(gram_rows, "row", root_index))
-    partner = jnp.concatenate(strips, axis=0)
-    square = lax.dot_general(
-        gram_rows, partner, (((1,), (1,)), ((), ())), preferred_element_type=jnp.float32
-    )
+    gram_cols = lax.all_gather(gram_tile, "row", axis=0, tiled=True)
+    square = jnp.dot(gram_rows, gram_cols, preferred_element_type=jnp.float32)
     poly_tile = (coef_cubic * gram_tile.astype(jnp.float32) + coef_quintic * square).astype(
         jnp.bfloat16
     )

time: 495 us -> 399 us (0.81)
  waiting for transfers between devices: 363 us -> 271 us
  other arithmetic: 22.3 us -> 17.1 us
    psum x1 -> x0, waiting for transfers between devices: 134 us -> none  [from_root(): return lax.psum(kept, axis)]
    all_gather x0 -> x1, waiting for transfers between devices: none -> 44.6 us  [per_device(): gram_cols = lax.all_gather(gram_tile, 'row', axis=0, tiled=True)]
    select_n x1 -> x0, other arithmetic: 5.09 us -> none  [from_root(): jnp.where(lax.axis_index(axis) == source, value, 0).astype(value.dtype)]
where the time goes in v1:
time: 399 us
  waiting for transfers between devices  271 us (68%)
  blocking collectives  68.7 us (17%)
  matrix products  27 us (7%)
  other arithmetic  17.1 us (4%)
  between operations  14.6 us (4%)
    reduce_scatter x1, waiting for transfers between devices, per_device(): lax.psum_scatter(lax.dot_general(ortho_column, ortho_tile, (((1,), (1,)),...  98.7 us
    psum x1, blocking collectives, per_device(): squares_total = lax.psum(jnp.sum(tile_wide * tile_wide), ('row', 'col'))  68.7 us
    all_gather x1, waiting for transfers between devices, per_device(): poly_rows = lax.all_gather(poly_tile, 'col', axis=1, tiled=True)  64.1 us
    all_gather x1, waiting for transfers between devices, per_device(): gram_rows = lax.all_gather(gram_tile, 'col', axis=1, tiled=True)  62.8 us
    all_gather x1, waiting for transfers between devices, per_device(): gram_cols = lax.all_gather(gram_tile, 'row', axis=0, tiled=True)  44.6 us
    convert_element_type x1, other arithmetic, per_device(): (column.astype(jnp.float32) * norm_scale).astype(jnp.bfloat16)  11.1 us
    dot_general x1, matrix products, per_device(): lax.dot_general(ortho_column, ortho_tile, (((1,), (1,)), ((), ())), prefe...  10.3 us
    dot_general x1, matrix products, per_device(): jnp.dot(poly_rows, ortho_column, preferred_element_type=jnp.float32)  9.4 us
  transfers between devices with their start and end apart: 5, of which 4 were waited for; matrix products, arithmetic and copies ran while one was open for 0% of the time, Pallas kernels for 0%

profile of v1, /device:TPU:1, one launch (start us, length us, event | category | flops | bytes accessed | tf_op | source)
XLA Modules:
  0.0 398.7 jit_solution(6731272440383303898)
XLA Ops:
  7.2 0.0 all-gather.5.cloned.1.call-start
  7.2 4.0 %multiply_reduce_fusion = (f32[]{:T(128)}, bf16[320,1024]{1,0:T(8,128)(2,1)}, f32[320,1024]{1,0:T(8,128)}) fusion(f32[320,1024]{1,0:T(8,128)} %param.2, f32[320,1024]{1,0:T(8,128)} %param.3), kind=kLoop, calls=%fused_computation.4 | loop fusion | flops 2621439 | bytes 4587524 | tf_op jit(solution)/shard_map/reduce_sum | solution.py:26
  11.2 0.0 all-gather.5.cloned.1.call-update
  11.3 0.0 reduce-scatter.2.cloned.1.call-start
  11.3 68.7 %psum.7 = f32[]{:T(128)} all-reduce(f32[]{:T(128)} %get-tuple-element.2), channel_id=1, replica_groups=mesh['row'=16,'col'=8] {'row','col'}, use_global_device_ids=true, to_apply=%region_1.0 | all-reduce | flops 1 | bytes 8 | tf_op jit(solution)/shard_map/psum | solution.py:26
  80.8 0.0 all-gather.5.cloned.1.call-done
  80.8 11.1 %multiply_convert_fusion = bf16[5120,1024]{1,0:T(8,128)(2,1)} fusion(bf16[5120,1024]{1,0:T(8,128)(2,1)} %all-gather.5.cloned.1.call-done, f32[]{:T(128)S(6)} %div.3), kind=kLoop, calls=%fused_computation | loop fusion | flops 15728640 | bytes 20971524 | tf_op jit(solution)/shard_map/convert_element_type | solution.py:28
  92.0 10.3 %fusion.4 = f32[5120,320]{0,1:T(8,128)} fusion(bf16[5120,1024]{1,0:T(8,128)(2,1)} %multiply_convert_fusion, s32[]{:T(128)S(6)} %select_n.3), kind=kOutput, calls=%fused_computation.10 | convolution fusion | flops 3355443200 | bytes 17694724 | tf_op jit(solution)/shard_map/dot_general | solution.py:33
  102.3 0.0 reduce-scatter.2.cloned.1.call-update
  102.3 0.0 all-gather.7.cloned.1.call-start
  102.4 98.7 %reduce-scatter.2.cloned.1.call-done = f32[640,320]{0,1:T(8,128)} async-done(((f32[5120,320]{0,1:T(8,128)}), f32[640,320]{0,1:T(8,128)}) %reduce-scatter.2.cloned.1.call-update) | async-done | bytes 819216 | tf_op jit(solution)/shard_map/reduce_scatter | solution.py:32
  201.1 1.9 convert_bitcast_fusion
  203.0 0.0 all-gather.7.cloned.1.call-update
  203.1 0.0 all-gather.9.cloned.1.call-start
  203.1 0.5 all-gather.9.cloned.1.call-update
  203.6 0.2 all-gather.11.cloned.1.call-start
  203.9 62.8 %all-gather.7.cloned.1.call-done = bf16[320,5120]{1,0:T(8,128)(2,1)} async-done(((bf16[320,640]{1,0:T(8,128)(2,1)}), bf16[320,5120]{1,0:T(8,128)(2,1)}) %all-gather.7.cloned.1.call-update) | async-done | bytes 3276816 | tf_op jit(solution)/shard_map/all_gather | solution.py:41
  266.7 44.6 %all-gather.9.cloned.1.call-done = bf16[5120,640]{1,0:T(8,128)(2,1)} async-done(((bf16[320,640]{1,0:T(8,128)(2,1)}), bf16[5120,640]{1,0:T(8,128)(2,1)}) %all-gather.9.cloned.1.call-update) | async-done | bytes 6553616 | tf_op jit(solution)/shard_map/all_gather | solution.py:42
  311.3 7.3 %fusion.3 = bf16[320,640]{1,0:T(8,128)(2,1)} fusion(bf16[320,5120]{1,0:T(8,128)(2,1)} %all-gather.7.cloned.1.call-done, bf16[5120,640]{1,0:T(8,128)(2,1)} %all-gather.9.cloned.1.call-done, bf16[320,640]{1,0:T(8,128)(2,1)} %convert_bitcast_fusion), kind=kOutput, calls=%fused_computation.9 | convolution fusion | flops 2098176000 | bytes 10649600 | tf_op jit(solution)/shard_map/dot_general | solution.py:43
  318.6 0.0 all-gather.11.cloned.1.call-update
  318.6 64.1 %all-gather.11.cloned.1.call-done = bf16[320,5120]{1,0:T(8,128)(2,1)} async-done(((bf16[320,640]{1,0:T(8,128)(2,1)}), bf16[320,5120]{1,0:T(8,128)(2,1)}) %all-gather.11.cloned.1.call-update) | async-done | bytes 3276816 | tf_op jit(solution)/shard_map/all_gather | solution.py:47
  382.8 9.4 %fusion.1 = bf16[320,1024]{1,0:T(8,128)(2,1)} fusion(bf16[320,5120]{1,0:T(8,128)(2,1)} %all-gather.11.cloned.1.call-done, bf16[5120,1024]{1,0:T(8,128)(2,1)} %multiply_convert_fusion, s32[]{:T(128)S(6)} %select_n.3), kind=kOutput, calls=%fused_computation.3 | convolution fusion | flops 3357081600 | bytes 15073284 | tf_op jit(solution)/shard_map/dot_general | solution.py:48
Async XLA Ops:
  7.2 73.7 %all-gather.5.cloned.1.call-start = ((), (), s32[]{:S(2)}) async-start(), calls=%async_computation.1 | async-start | bytes 11141120 | tf_op jit(solution)/shard_map/all_gather | solution.py:24
  11.3 189.8 %reduce-scatter.2.cloned.1.call-start = ((), (), s32[]{:S(2)}) async-start(), calls=%async_computation.2 | async-start | bytes 7372800 | tf_op jit(solution)/shard_map/reduce_scatter | solution.py:32
  102.3 164.4 %all-gather.7.cloned.1.call-start = ((), (), s32[]{:S(2)}) async-start(), calls=%async_computation.3 | async-start | bytes 3686400 | tf_op jit(solution)/shard_map/all_gather | solution.py:41
  203.1 108.2 %all-gather.9.cloned.1.call-start = ((), (), s32[]{:S(2)}) async-start(), calls=%async_computation.4 | async-start | bytes 6963200 | tf_op jit(solution)/shard_map/all_gather | solution.py:42
  203.6 179.1 %all-gather.11.cloned.1.call-start = ((), (), s32[]{:S(2)}) async-start(), calls=%async_computation.5 | async-start | bytes 3686400 | tf_op jit(solution)/shard_map/all_gather | solution.py:47
Sparse Core Ops, SparseCore 0:
  11.4 66.8 all-gather.4
  102.4 98.6 reduce-scatter.1
  204.3 62.3 all-gather.6
  269.0 42.3 all-gather.8
  318.7 63.9 all-gather.10

commit v2 on v1

v2 whole, which is shorter than its diff:
```python
import math

import jax
import jax.numpy as jnp
from jax import lax
from jax.experimental import pallas as pl
from jax.experimental.pallas import tpu as pltpu
from jax.sharding import PartitionSpec as P

momentum_decay = 0.95
target_rms = 0.25
norm_epsilon = 1e-07
coef_linear = 3.4445
coef_cubic = -4.775
coef_quintic = 2.0315

MESH = pl.DeviceIdType.MESH
F32 = jnp.float32
BF16 = jnp.bfloat16

TILE = 320
BLOCK = 640
WIDTH = 1024
PIECE = 80


class Gather:
    def __init__(self, own, whole, half, p, b, right, left, pair, send, recv):
        def copy(n, src, dst, device):
            return pltpu.make_async_remote_copy(
                src, dst, send.at[n], recv.at[n], device_id=device, device_id_type=MESH
            )

        lo, hi = lax.rem(p + 3, 4), lax.rem(p + 1, 4)
        c = 1 - b
        own_place = whole(p, b)
        self.pair = copy(0, own, own_place, pair)
        self.right = copy(1, own, own_place, right)
        self.left = copy(2, own, own_place, left)
        self.right_pair = copy(3, whole(p, c), whole(p, c), right)
        self.left_pair = copy(4, whole(p, c), whole(p, c), left)
        self.on_right = copy(5, half(lo, b, 0), half(lo, b, 0), right)
        self.on_left = copy(6, half(hi, b, 1), half(hi, b, 1), left)
        self.on_right_pair = copy(7, half(lo, c, 0), half(lo, c, 0), right)
        self.on_left_pair = copy(8, half(hi, c, 1), half(hi, c, 1), left)
        opp = lax.rem(p + 2, 4)
        self.order = [(p, b), (p, c), (lo, b), (hi, b), (lo, c), (hi, c), (opp, b), (opp, c)]

    def start(self):
        self.pair.start()
        self.right.start()
        self.left.start()

    def arrive(self, n):
        if n == 1:
            self.pair.wait_recv()
            self.right_pair.start()
            self.left_pair.start()
        elif n == 2:
            self.right.wait_recv()
            self.on_right.start()
        elif n == 3:
            self.left.wait_recv()
            self.on_left.start()
        elif n == 4:
            self.right_pair.wait_recv()
            self.on_right_pair.start()
        elif n == 5:
            self.left_pair.wait_recv()
            self.on_left_pair.start()
        elif n == 6:
            self.on_right.wait_recv()
            self.on_left.wait_recv()
        elif n == 7:
            self.on_right_pair.wait_recv()
            self.on_left_pair.wait_recv()

    def finish(self):
        for c in (
            self.pair, self.right, self.left, self.right_pair, self.left_pair,
            self.on_right, self.on_left, self.on_right_pair, self.on_left_pair,
        ):
            c.wait_send()


def kernel(
    blended, out,
    raw, ortho, part, hop_half, hop_whole, hop_pair, gram_cols, gram_rows, poly, square, total, sums,
    b_send, b_recv, bs_send, bs_recv, half_send, half_recv, whole_send, whole_recv, z_send, z_recv,
    gr_send, gr_recv, gc_send, gc_recv, gs_send, gs_recv, p_send, p_recv, ps_send, ps_recv,
    sum_send, sum_recv,
):
    row, col = lax.axis_index("row"), lax.axis_index("col")
    core = lax.rem(row, 2)
    x = lax.rem(lax.div(row, 2), 4)
    z_lo = lax.div(row, 8)
    y, z_hi = lax.div(col, 2), lax.rem(col, 2)
    chip_row = lax.div(row, 2)

    def at(x=x, y=y, z_lo=z_lo, z_hi=z_hi, core=core):
        return ((z_lo * 4 + x) * 2 + core, y * 2 + z_hi)

    def turn(v, n):
        return lax.rem(v + n, 4)

    sibling = at(core=1 - core)
    x_right, x_left = at(x=turn(x, 1)), at(x=turn(x, 3))
    y_right, y_left = at(y=turn(y, 1)), at(y=turn(y, 3))
    lo_pair, hi_pair = at(z_lo=1 - z_lo), at(z_hi=1 - z_hi)
    z = z_hi * 2 + z_lo
    peers = {
        "core": [sibling],
        "x": [at(x=turn(x, n)) for n in (1, 2, 3)],
        "y": [at(y=turn(y, n)) for n in (1, 2, 3)],
        "z": [at(z_lo=lax.rem(turn(z, n), 2), z_hi=lax.div(turn(z, n), 2)) for n in (1, 2, 3)],
    }
    everyone = [d for group in peers.values() for d in group]

    barrier = pltpu.get_barrier_semaphore()
    for d in everyone:
        pl.semaphore_signal(barrier, inc=1, device_id=d, device_id_type=MESH)
    pl.semaphore_wait(barrier, len(everyone))

    gather_b = Gather(
        blended,
        lambda p, b: raw.at[b * 4 + p],
        lambda p, b, k: raw.at[b * 4 + p, pl.ds(k * 160, 160)],
        x, z_lo, x_right, x_left, lo_pair, b_send, b_recv,
    )
    gather_b.start()

    mine = jnp.zeros((8, 128), F32)
    for k in range(8):
        wide = blended[:, k * 128 : (k + 1) * 128].astype(F32).reshape(TILE // 8, 8, 128)
        mine = mine + jnp.sum(wide * wide, axis=0)
    for stage, (place, size) in enumerate(((core, 2), (x, 4), (y, 4), (z, 4))):
        group = list(peers.values())[stage]
        sums[stage, place] = mine
        copies = [
            pltpu.make_async_remote_copy(
                sums.at[stage, place], sums.at[stage, place],
                sum_send.at[stage, n], sum_recv.at[stage, n], device_id=d, device_id_type=MESH,
            )
            for n, d in enumerate(group)
        ]
        for c in copies:
            c.start()
        for c in copies:
            c.wait()
        mine = sums[stage, 0]
        for n in range(1, size):
            mine = mine + sums[stage, n]
    squares_total = jnp.sum(mine, keepdims=True)
    norm_scale = target_rms * math.sqrt(5120) / (jnp.sqrt(squares_total) + norm_epsilon)

    def to_sibling(n, src, send, recv):
        return pltpu.make_async_remote_copy(
            src, src, send.at[n], recv.at[n], device_id=sibling, device_id_type=MESH
        )

    mine_rows = pl.ds(pl.multiple_of(y * PIECE, PIECE), PIECE)

    def scale(src, j):
        def body(k, carry):
            rows = pl.ds(pl.multiple_of(k * 32, 32), 32)
            ortho[j, core, rows] = (src[rows].astype(F32) * norm_scale).astype(BF16)
            return carry

        lax.fori_loop(0, TILE // 32, body, 0)

    def partial(p, b):
        part[b, p] = lax.dot_general(
            ortho[b * 4 + p, core],
            ortho[chip_row].reshape(BLOCK, WIDTH),
            (((1,), (1,)), ((), ())),
            preferred_element_type=F32,
        )

    def half_hops(n, p, b):
        far = turn(y, 2) * PIECE
        return [
            pltpu.make_async_remote_copy(
                part.at[b, p, pl.ds(pl.multiple_of(far + 40 * k, 8), 40)],
                hop_half.at[n, k],
                half_send.at[n, k], half_recv.at[n, k], device_id=d, device_id_type=MESH,
            )
            for k, d in enumerate((y_right, y_left))
        ]

    def whole_hops(n, p, b):
        return [
            pltpu.make_async_remote_copy(
                part.at[b, p, pl.ds(pl.multiple_of(near * PIECE, 8), PIECE)],
                hop_whole.at[n, k],
                whole_send.at[n, k], whole_recv.at[n, k], device_id=d, device_id_type=MESH,
            )
            for k, (near, d) in enumerate(((turn(y, 1), y_right), (turn(y, 3), y_left)))
        ]

    def pair_hop(n, p):
        return pltpu.make_async_remote_copy(
            part.at[1 - z_hi, p, mine_rows], hop_pair.at[n],
            z_send.at[n], z_recv.at[n], device_id=hi_pair, device_id_type=MESH,
        )

    order = gather_b.order

    def reduce_1(n):
        for c in half_hops(n, *order[n]):
            c.start()

    def reduce_2(n):
        p, b = order[n]
        halves, wholes = half_hops(n, p, b), whole_hops(n, p, b)
        for k, near in enumerate((turn(y, 1), turn(y, 3))):
            halves[k].wait_recv()
            rows = pl.ds(pl.multiple_of(near * PIECE + 40 * k, 8), 40)
            part[b, p, rows] = part[b, p, rows] + hop_half[n, k]
            wholes[k].start()

    def reduce_3(n):
        p, b = order[n]
        for c in whole_hops(n, p, b):
            c.wait_recv()
        part[b, p, mine_rows] = part[b, p, mine_rows] + (hop_whole[n, 0] + hop_whole[n, 1])

    twos = ((0, 1), (2, 4), (3, 5), (6, 7))

    def reduce_4(m):
        pair_hop(m, order[twos[m][0]][0]).start()

    def reduce_5(m):
        p = order[twos[m][0]][0]
        pair_hop(m, p).wait_recv()
        tile = (part[z_hi, p, mine_rows] + hop_pair[m]).astype(BF16)
        gram_cols[z_hi, p, core, y] = tile
        gram_rows[chip_row, pl.ds(pl.multiple_of(p * PIECE, 16), PIECE)] = tile

    def own_block():
        scale(blended, chip_row)
        to_sibling(0, ortho.at[chip_row, core], bs_send, bs_recv).start()
        to_sibling(0, ortho.at[chip_row, core], bs_send, bs_recv).wait_recv()

    for n in range(11):
        if n < 8:
            p, b = order[n]
            gather_b.arrive(n)
            if n == 0:
                own_block()
            else:
                scale(raw.at[b * 4 + p], b * 4 + p)
                to_sibling(n, ortho.at[b * 4 + p, core], bs_send, bs_recv).start()
            partial(p, b)
            reduce_1(n)
        if 1 <= n < 9:
            reduce_2(n - 1)
        if 2 <= n < 10:
            reduce_3(n - 2)
            for m, (_, second) in enumerate(twos):
                if second == n - 2:
                    reduce_4(m)
        if 3 <= n:
            for m, (_, second) in enumerate(twos):
                if second == n - 3:
                    reduce_5(m)

    def rows_half(p, b, k):
        return gram_rows.at[b * 4 + p, pl.ds(k * 160, 160)]

    gather_rows = Gather(
        gram_rows.at[chip_row], lambda p, b: gram_rows.at[b * 4 + p], rows_half,
        x, z_lo, x_right, x_left, lo_pair, gr_send, gr_recv,
    )
    gather_cols = Gather(
        gram_cols.at[z_hi, :, core, y],
        lambda p, b: gram_cols.at[b, :, core, p],
        lambda p, b, k: gram_cols.at[b, pl.ds(k * 2, 2), core, p],
        y, z_hi, y_right, y_left, hi_pair, gc_send, gc_recv,
    )
    gather_cols.start()
    gather_rows.start()

    def cols_to_sibling(n):
        p, b = gather_cols.order[n]
        return to_sibling(n, gram_cols.at[b, :, core, p], gs_send, gs_recv)

    for n in range(8):
        gather_cols.arrive(n)
        cols_to_sibling(n).start()
        gather_rows.arrive(n)
    for n in range(8):
        cols_to_sibling(n).wait_recv()

    square[...] = jnp.zeros_like(square)

    def add_square(k, carry):
        right = gram_cols[lax.div(k, 4), lax.rem(k, 4)].reshape(BLOCK, BLOCK)
        square[...] += jnp.dot(gram_rows[k], right, preferred_element_type=F32)
        return carry

    lax.fori_loop(0, 8, add_square, 0)
    poly[col, core] = (
        coef_cubic * gram_rows[chip_row].astype(F32) + coef_quintic * square[...]
    ).astype(BF16)

    gather_p = Gather(
        poly.at[col, core],
        lambda p, b: poly.at[p * 2 + b, core],
        lambda p, b, k: poly.at[p * 2 + b, core, pl.ds(k * 160, 160)],
        y, z_hi, y_right, y_left, hi_pair, p_send, p_recv,
    )
    gather_p.start()

    def poly_to_sibling(n):
        p, b = gather_p.order[n]
        return to_sibling(n, poly.at[p * 2 + b, core], ps_send, ps_recv)

    for n in range(1, 8):
        p, b = order[n]
        to_sibling(n, ortho.at[b * 4 + p, core], bs_send, bs_recv).wait_recv()

    lanes = pl.ds(pl.multiple_of(core * 256, 128), 384)
    total[...] = jnp.zeros_like(total)

    def add_product(p, b):
        def body(a, carry):
            left = poly[p * 2 + b, a, :, lanes]
            first = pl.multiple_of(p * PIECE, 16)
            right = jnp.concatenate(
                [ortho[b * 4 + k, a, pl.ds(first, PIECE)] for k in range(4)], axis=0
            )
            total[...] += lax.dot_general(
                left, right, (((0,), (0,)), ((), ())), preferred_element_type=F32
            )
            return carry

        lax.fori_loop(0, 2, body, 0)

    for n in range(8):
        gather_p.arrive(n)
        poly_to_sibling(n).start()
        poly_to_sibling(n).wait_recv()
        add_product(*gather_p.order[n])

    product = total[pl.ds(pl.multiple_of(core * 64, 8), TILE)]
    out[...] = (
        math.sqrt(8192) * (coef_linear * ortho[chip_row, core].astype(F32) + product)
    ).astype(BF16)

    for g in (gather_b, gather_rows, gather_cols, gather_p):
        g.finish()
    for n in range(8):
        p, b = order[n]
        to_sibling(n, ortho.at[b * 4 + p, core], bs_send, bs_recv).wait_send()
        cols_to_sibling(n).wait_send()
        poly_to_sibling(n).wait_send()
        for c in half_hops(n, p, b) + whole_hops(n, p, b):
            c.wait_send()
    for m in range(4):
        pair_hop(m, order[twos[m][0]][0]).wait_send()


def iterate(blended):
    dma = pltpu.SemaphoreType.DMA
    return pl.pallas_call(
        kernel,
        out_shape=jax.ShapeDtypeStruct((TILE, WIDTH), BF16),
        in_specs=[pl.BlockSpec(memory_space=pltpu.VMEM)],
        out_specs=pl.BlockSpec(memory_space=pltpu.VMEM),
        scratch_shapes=[
            pltpu.VMEM((8, TILE, WIDTH), BF16),
            pltpu.VMEM((8, 2, TILE, WIDTH), BF16),
            pltpu.VMEM((2, 4, TILE, BLOCK), F32),
            pltpu.VMEM((8, 2, 40, BLOCK), F32),
            pltpu.VMEM((8, 2, PIECE, BLOCK), F32),
            pltpu.VMEM((4, PIECE, BLOCK), F32),
            pltpu.VMEM((2, 4, 2, 4, PIECE, BLOCK), BF16),
            pltpu.VMEM((8, TILE, BLOCK), BF16),
            pltpu.VMEM((8, 2, TILE, BLOCK), BF16),
            pltpu.VMEM((TILE, BLOCK), F32),
            pltpu.VMEM((384, WIDTH), F32),
            pltpu.VMEM((4, 4, 8, 128), F32),
            dma((9,)), dma((9,)), dma((8,)), dma((8,)),
            dma((8, 2)), dma((8, 2)), dma((8, 2)), dma((8, 2)), dma((4,)), dma((4,)),
            dma((9,)), dma((9,)), dma((9,)), dma((9,)), dma((8,)), dma((8,)),
            dma((9,)), dma((9,)), dma((8,)), dma((8,)),
            dma((4, 3)), dma((4, 3)),
        ],
        compiler_params=pltpu.CompilerParams(
            collective_id=0, has_side_effects=True, vmem_limit_bytes=60 << 20
        ),
    )(blended)


def per_device(grad, momentum):
    new_momentum = momentum_decay * momentum + grad
    blended = (grad + momentum_decay * new_momentum).astype(BF16)
    return (iterate(blended), new_momentum)


def solution(mesh):
    placed = (P("row", "col"), P("row", "col"))
    return jax.shard_map(
        per_device,
        mesh=mesh,
        in_specs=placed,
        out_specs=(P("row", "col"), P("row", "col")),
        check_vma=False,
    )
```

time: 399 us -> 181 us (0.45)
  waiting for transfers between devices: 271 us -> 0 us
  Pallas kernels: 0 us -> 175 us
  blocking collectives: 68.7 us -> 0 us
  matrix products: 27 us -> 0 us
  between operations: 14.6 us -> 0.64 us
  other arithmetic: 17.1 us -> 3.42 us
    pallas_call x0 -> x1, Pallas kernels: none -> 175 us  [iterate(): pl.pallas_call(kernel, out_shape=jax.ShapeDtypeStruct((TILE, WIDTH), BF16...]
    all_gather x4 -> x0, waiting for transfers between devices: 172 us -> none  [the longest x1 64.1 us: per_device(): poly_rows = lax.all_gather(poly_tile, 'col', axis=1, tiled=True)]
    reduce_scatter x1 -> x0, waiting for transfers between devices: 98.7 us -> none  [per_device(): lax.psum_scatter(lax.dot_general(ortho_column, ortho_tile, (((1,), (1,)),...]
    psum x1 -> x0, blocking collectives: 68.7 us -> none  [per_device(): squares_total = lax.psum(jnp.sum(tile_wide * tile_wide), ('row', 'col'))]
    dot_general x3 -> x0, matrix products: 27 us -> none  [the longest x1 10.3 us: per_device(): lax.dot_general(ortho_column, ortho_tile, (((1,), (1,)), ((), ())), prefe...]
    convert_element_type x2 -> x1, other arithmetic: 13.1 us -> 3.42 us  [per_device(): blended = (grad + momentum_decay * new_momentum).astype(BF16)]
    reduce_sum x1 -> x0, other arithmetic: 4.02 us -> none  [per_device(): squares_total = lax.psum(jnp.sum(tile_wide * tile_wide), ('row', 'col'))]
  transfers between devices with their start and end apart: 5 -> 0, of which waited for: 4 -> 0; matrix products, arithmetic and copies ran while one was open for 0% -> 0% of each run, Pallas kernels for 0% -> 0%
where the time goes in v2:
time: 181 us
  Pallas kernels  175 us (97%)
  other arithmetic  3.42 us (2%)
  local copies, waits for them, and re-layouts  1.97 us (1%)
    pallas_call x1, Pallas kernels, iterate(): pl.pallas_call(kernel, out_shape=jax.ShapeDtypeStruct((TILE, WIDTH), BF16...  175 us

profile of v2, /device:TPU:1, one launch (start us, length us, event | category | flops | bytes accessed | tf_op | source)
XLA Modules:
  0.0 180.9 jit_solution(7658408938122152479)
XLA Ops:
  0.6 3.4 %add_convert_fusion = (bf16[320,1024]{1,0:T(8,128)(2,1)}, f32[320,1024]{1,0:T(8,128)}) fusion(f32[320,1024]{1,0:T(8,128)} %param.2, f32[320,1024]{1,0:T(8,128)} %param.3), kind=kLoop, calls=%fused_computation | loop fusion | flops 1638400 | bytes 4587520 | tf_op jit(solution)/shard_map/convert_element_type | solution.py:397
  4.0 174.9 %shard_map.41 = bf16[320,1024]{1,0:T(8,128)(2,1)} custom-call(bf16[320,1024]{1,0:T(8,128)(2,1)} %get-tuple-element.2.blended), custom_call_target="tpu_custom_call" | custom-call | tf_op jit(solution)/shard_map/pallas_call | solution.py:365
  179.0 2.0 %copy.5 = bf16[320,1024]{1,0:T(8,128)(2,1)} copy(bf16[320,1024]{1,0:T(8,128)(2,1)} %shard_map.41) | data formatting | bytes 1310720

commit v3 on v2

v3 whole, which is shorter than its diff:
```python
import math

import jax
import jax.numpy as jnp
from jax import lax
from jax.experimental import pallas as pl
from jax.experimental.pallas import tpu as pltpu
from jax.sharding import PartitionSpec as P

momentum_decay = 0.95
target_rms = 0.25
norm_epsilon = 1e-07
coef_linear = 3.4445
coef_cubic = -4.775
coef_quintic = 2.0315

MESH = pl.DeviceIdType.MESH
F32 = jnp.float32
BF16 = jnp.bfloat16

TILE = 320
BLOCK = 640
WIDTH = 1024
PIECE = 80


class Gather:
    def __init__(self, own, whole, some, rows, cut, p, b, right, left, pair, send, recv, across=0, cut_pair=None):
        def copy(n, src, dst, device):
            return pltpu.make_async_remote_copy(
                src, dst, send.at[n], recv.at[n], device_id=device, device_id_type=MESH
            )

        def on(n, p, b, first, size, device):
            place = some(p, b, first, size)
            return copy(n, place, place, device)

        lo, hi = lax.rem(p + 3, 4), lax.rem(p + 1, 4)
        opp = lax.rem(p + 2, 4)
        c = 1 - b
        own_place = whole(p, b)
        around = rows - across
        cut_pair = cut if cut_pair is None else cut_pair
        self.pair = copy(0, own, own_place, pair)
        self.right = copy(1, own, own_place, right)
        self.left = copy(2, own, own_place, left)
        self.right_pair = on(3, p, c, 0, around, right)
        self.left_pair = on(4, p, c, 0, around, left)
        self.on_right = on(5, lo, b, 0, cut, right)
        self.on_left = on(6, hi, b, cut, rows - cut, left)
        self.on_right_pair = on(7, lo, c, 0, cut_pair, right)
        self.on_left_pair = on(8, hi, c, cut_pair, around - cut_pair, left)
        self.all = [
            self.pair, self.right, self.left, self.right_pair, self.left_pair,
            self.on_right, self.on_left, self.on_right_pair, self.on_left_pair,
        ]
        self.across = []
        if across:
            self.across = [on(9 + k, q, b, around, across, pair) for k, q in enumerate((lo, hi, opp))]
            self.all = self.all + self.across
        self.order = [(p, b), (p, c), (lo, b), (hi, b), (lo, c), (hi, c), (opp, b), (opp, c)]

    def start(self):
        self.pair.start()
        self.right.start()
        self.left.start()

    def arrive(self, n):
        waits = {
            1: [self.pair], 2: [self.right], 3: [self.left], 4: [self.right_pair], 5: [self.left_pair],
            6: [self.on_right, self.on_left], 7: [self.on_right_pair, self.on_left_pair],
        }
        starts = {
            1: [self.right_pair, self.left_pair], 2: [self.on_right], 3: [self.on_left],
            4: [self.on_right_pair], 5: [self.on_left_pair],
        }
        if self.across:
            for block, k in ((2, 0), (3, 1), (6, 2)):
                starts[block] = starts.get(block, []) + [self.across[k]]
        for c in waits[n]:
            c.wait_recv()
        for c in starts.get(n, []):
            c.start()

    def arrive_across(self, n):
        if self.across:
            self.across[{4: 0, 5: 1, 7: 2}[n]].wait_recv()

    def finish(self):
        for c in self.all:
            c.wait_send()


def kernel(
    blended, out,
    raw, ortho, part, hop_half, hop_whole, hop_plane, hop_pair, gram_cols, gram_rows, poly, square, total, sums,
    b_send, b_recv, bs_send, bs_recv, half_send, half_recv, whole_send, whole_recv, plane_send, plane_recv, z_send, z_recv,
    gr_send, gr_recv, gc_send, gc_recv, gs_send, gs_recv, p_send, p_recv, ps_send, ps_recv,
    sum_send, sum_recv,
):
    row, col = lax.axis_index("row"), lax.axis_index("col")
    core = lax.rem(row, 2)
    x = lax.rem(lax.div(row, 2), 4)
    z_lo = lax.div(row, 8)
    y, z_hi = lax.div(col, 2), lax.rem(col, 2)
    chip_row = lax.div(row, 2)

    def at(x=x, y=y, z_lo=z_lo, z_hi=z_hi, core=core):
        return ((z_lo * 4 + x) * 2 + core, y * 2 + z_hi)

    def turn(v, n):
        return lax.rem(v + n, 4)

    sibling = at(core=1 - core)
    x_right, x_left = at(x=turn(x, 1)), at(x=turn(x, 3))
    y_right, y_left = at(y=turn(y, 1)), at(y=turn(y, 3))
    lo_pair, hi_pair = at(z_lo=1 - z_lo), at(z_hi=1 - z_hi)
    z = z_hi * 2 + z_lo
    peers = {
        "core": [sibling],
        "x": [at(x=turn(x, n)) for n in (1, 2, 3)],
        "y": [at(y=turn(y, n)) for n in (1, 2, 3)],
        "z": [at(z_lo=lax.rem(turn(z, n), 2), z_hi=lax.div(turn(z, n), 2)) for n in (1, 2, 3)],
    }
    everyone = [d for group in peers.values() for d in group]

    barrier = pltpu.get_barrier_semaphore()
    for d in everyone:
        pl.semaphore_signal(barrier, inc=1, device_id=d, device_id_type=MESH)
    pl.semaphore_wait(barrier, len(everyone))

    gather_b = Gather(
        blended,
        lambda p, b: raw.at[b * 4 + p],
        lambda p, b, first, rows: raw.at[b * 4 + p, pl.ds(first, rows)],
        TILE, 160, x, z_lo, x_right, x_left, lo_pair, b_send, b_recv,
    )
    gather_b.start()

    mine = jnp.zeros((8, 128), F32)
    for k in range(8):
        wide = blended[:, k * 128 : (k + 1) * 128].astype(F32).reshape(TILE // 8, 8, 128)
        mine = mine + jnp.sum(wide * wide, axis=0)
    for stage, (place, size) in enumerate(((core, 2), (x, 4), (y, 4), (z, 4))):
        group = list(peers.values())[stage]
        sums[stage, place] = mine
        copies = [
            pltpu.make_async_remote_copy(
                sums.at[stage, place], sums.at[stage, place],
                sum_send.at[stage, n], sum_recv.at[stage, n], device_id=d, device_id_type=MESH,
            )
            for n, d in enumerate(group)
        ]
        for c in copies:
            c.start()
        for c in copies:
            c.wait()
        mine = sums[stage, 0]
        for n in range(1, size):
            mine = mine + sums[stage, n]
    squares_total = jnp.sum(mine, keepdims=True)
    norm_scale = target_rms * math.sqrt(5120) / (jnp.sqrt(squares_total) + norm_epsilon)

    def to_sibling(n, src, send, recv):
        return pltpu.make_async_remote_copy(
            src, src, send.at[n], recv.at[n], device_id=sibling, device_id_type=MESH
        )

    mine_rows = pl.ds(pl.multiple_of(y * PIECE, PIECE), PIECE)

    def scale(src, j):
        def body(k, carry):
            rows = pl.ds(pl.multiple_of(k * 32, 32), 32)
            ortho[j, core, rows] = (src[rows].astype(F32) * norm_scale).astype(BF16)
            return carry

        lax.fori_loop(0, TILE // 32, body, 0)

    def partial(p, b):
        part[b, p] = lax.dot_general(
            ortho[b * 4 + p, core],
            ortho[chip_row].reshape(BLOCK, WIDTH),
            (((1,), (1,)), ((), ())),
            preferred_element_type=F32,
        )

    def half_hops(n, p, b):
        far = turn(y, 2) * PIECE
        return [
            pltpu.make_async_remote_copy(
                part.at[b, p, pl.ds(pl.multiple_of(far + 40 * k, 8), 40)],
                hop_half.at[n, k],
                half_send.at[n, k], half_recv.at[n, k], device_id=d, device_id_type=MESH,
            )
            for k, d in enumerate((y_right, y_left))
        ]

    def whole_hops(n, p, b):
        return [
            pltpu.make_async_remote_copy(
                part.at[b, p, pl.ds(pl.multiple_of(near * PIECE, 8), PIECE)],
                hop_whole.at[n, k],
                whole_send.at[n, k], whole_recv.at[n, k], device_id=d, device_id_type=MESH,
            )
            for k, (near, d) in enumerate(((turn(y, 1), y_right), (turn(y, 3), y_left)))
        ]

    order = gather_b.order
    lo, hi, opp = turn(x, 3), turn(x, 1), turn(x, 2)
    places = (x, lo, hi, opp)

    def plane_hop(m):
        return pltpu.make_async_remote_copy(
            part.at[1 - z_hi, places[m]], hop_plane.at[m],
            plane_send.at[m], plane_recv.at[m], device_id=hi_pair, device_id_type=MESH,
        )

    def pair_hop(m):
        return pltpu.make_async_remote_copy(
            part.at[1 - z_hi, places[m], mine_rows], hop_pair.at[m - 2],
            z_send.at[m - 2], z_recv.at[m - 2], device_id=hi_pair, device_id_type=MESH,
        )

    tasks = ((x, z_hi), (lo, z_hi), (hi, z_lo), (hi, 1 - z_lo), (opp, z_lo), (opp, 1 - z_lo))

    def reduce_1(t):
        for c in half_hops(t, *tasks[t]):
            c.start()

    def reduce_2(t):
        p, b = tasks[t]
        halves, wholes = half_hops(t, p, b), whole_hops(t, p, b)
        for k, near in enumerate((turn(y, 1), turn(y, 3))):
            halves[k].wait_recv()
            rows = pl.ds(pl.multiple_of(near * PIECE + 40 * k, 8), 40)
            part[b, p, rows] = part[b, p, rows] + hop_half[t, k]
            wholes[k].start()

    def reduce_3(t):
        p, b = tasks[t]
        for c in whole_hops(t, p, b):
            c.wait_recv()
        part[b, p, mine_rows] = part[b, p, mine_rows] + (hop_whole[t, 0] + hop_whole[t, 1])

    def add_planes(m):
        plane_hop(m).wait_recv()
        part[z_hi, places[m]] = part[z_hi, places[m]] + hop_plane[m]
        reduce_1(m)

    def finish_tile(m):
        p = places[m]
        tile = part[z_hi, p, mine_rows]
        if m >= 2:
            pair_hop(m).wait_recv()
            tile = tile + hop_pair[m - 2]
        tile = tile.astype(BF16)
        gram_cols[z_hi, p, core, y] = tile
        gram_rows[chip_row, pl.ds(pl.multiple_of(p * PIECE, 16), PIECE)] = tile

    def from_sibling(n):
        p, b = order[n]
        return to_sibling(n, ortho.at[b * 4 + p, core], bs_send, bs_recv)

    def process(n):
        p, b = order[n]
        scale(blended if n == 0 else raw.at[b * 4 + p], b * 4 + p)
        from_sibling(n).start()
        if n == 0:
            from_sibling(0).wait_recv()
        partial(p, b)

    def gather_rows(m):
        def place(p, b, first, rows):
            part_of = turn(p, (0, 3, 1, 2)[m]) * PIECE
            return gram_rows.at[b * 4 + p, pl.ds(pl.multiple_of(part_of + first, 16), rows)]

        return Gather(
            place(x, z_lo, 0, PIECE), lambda p, b: place(p, b, 0, PIECE), place,
            PIECE, 48, x, z_lo, x_right, x_left, lo_pair, gr_send.at[m], gr_recv.at[m],
        )

    def gather_cols(m):
        q = turn(x, (0, 3, 1, 2)[m])

        def place(p, b, first, rows):
            return gram_cols.at[b, q, core, p, pl.ds(first, rows)]

        return Gather(
            place(y, z_hi, 0, PIECE), lambda p, b: place(p, b, 0, PIECE), place,
            PIECE, 48, y, z_hi, y_right, y_left, hi_pair, gc_send.at[m], gc_recv.at[m],
        )

    def cols_to_sibling(m, n):
        p, b = cols_gathers[m].order[n]
        place = gram_cols.at[b, turn(x, (0, 3, 1, 2)[m]), core, p]
        return to_sibling(n, place, gs_send.at[m], gs_recv.at[m])

    rows_gathers = [gather_rows(m) for m in range(4)]
    cols_gathers = [gather_cols(m) for m in range(4)]

    def spread(m, event):
        if event == 0:
            finish_tile(m)
            cols_gathers[m].start()
            rows_gathers[m].start()
            cols_to_sibling(m, 0).start()
        for n in ((), (1, 2, 3), (4, 5), (6, 7))[event]:
            cols_gathers[m].arrive(n)
            cols_to_sibling(m, n).start()
            rows_gathers[m].arrive(n)

    process(0)
    for n in (1, 2, 3):
        gather_b.arrive(n)
    process(1)
    plane_hop(0).start()
    process(3)
    reduce_1(2)
    process(2)
    reduce_2(2)
    gather_b.arrive(4)
    gather_b.arrive(5)
    process(4)
    plane_hop(1).start()
    process(5)
    reduce_1(3)
    reduce_3(2)
    add_planes(0)
    reduce_2(3)
    gather_b.arrive(6)
    process(6)
    reduce_1(4)
    reduce_2(0)
    reduce_3(3)
    pair_hop(2).start()
    gather_b.arrive(7)
    process(7)
    reduce_1(5)
    reduce_2(4)
    reduce_3(0)
    spread(0, 0)
    reduce_2(5)
    spread(2, 0)
    add_planes(1)
    reduce_3(4)
    spread(0, 1)
    reduce_3(5)
    pair_hop(3).start()
    spread(2, 1)
    reduce_2(1)
    spread(0, 2)
    spread(2, 2)
    spread(3, 0)
    reduce_3(1)
    spread(1, 0)
    spread(0, 3)
    spread(2, 3)
    spread(3, 1)
    spread(1, 1)
    spread(3, 2)
    spread(1, 2)
    spread(3, 3)
    spread(1, 3)
    for m in range(4):
        for n in range(8):
            cols_to_sibling(m, n).wait_recv()

    def half_of_poly(h):
        rows = pl.ds(h * 160, 160)
        square[...] = jnp.zeros_like(square)

        def add_square(k, carry):
            right = gram_cols[lax.div(k, 4), lax.rem(k, 4)].reshape(BLOCK, BLOCK)
            square[...] += jnp.dot(gram_rows[k, rows], right, preferred_element_type=F32)
            return carry

        lax.fori_loop(0, 8, add_square, 0)
        poly[col, h, core] = (
            coef_cubic * gram_rows[chip_row, rows].astype(F32) + coef_quintic * square[...]
        ).astype(BF16)

    gathers_p = [
        Gather(
            poly.at[col, h, core],
            lambda p, b, h=h: poly.at[p * 2 + b, h, core],
            lambda p, b, first, rows, h=h: poly.at[p * 2 + b, h, core, pl.ds(first, rows)],
            160, 80, y, z_hi, y_right, y_left, hi_pair, p_send.at[h], p_recv.at[h], across=64, cut_pair=48,
        )
        for h in range(2)
    ]

    def poly_to_sibling(h, n):
        p, b = gathers_p[h].order[n]
        return to_sibling(n, poly.at[p * 2 + b, h, core], ps_send.at[h], ps_recv.at[h])

    for h in range(2):
        half_of_poly(h)
        gathers_p[h].start()
        poly_to_sibling(h, 0).start()

    for n in range(1, 8):
        from_sibling(n).wait_recv()

    lanes = pl.ds(pl.multiple_of(core * 256, 128), 384)
    total[...] = jnp.zeros_like(total)

    def add_product(h, n):
        poly_to_sibling(h, n).wait_recv()
        p, b = gathers_p[h].order[n]
        first = pl.multiple_of(p * PIECE, 16)
        left = poly[p * 2 + b, h, :, :, lanes].reshape(TILE, 384)
        right = jnp.concatenate(
            [ortho[b * 4 + 2 * h + k, a, pl.ds(first, PIECE)] for a in range(2) for k in range(2)], axis=0
        )
        total[...] += lax.dot_general(
            left, right, (((0,), (0,)), ((), ())), preferred_element_type=F32
        )

    for h in range(2):
        for n in (1, 2, 3):
            gathers_p[h].arrive(n)
            poly_to_sibling(h, n).start()
    for h in range(2):
        for n in range(4):
            add_product(h, n)
    for h in range(2):
        gathers_p[h].arrive(6)
        poly_to_sibling(h, 6).start()
        for n in (4, 5):
            gathers_p[h].arrive(n)
        for n in (4, 5):
            gathers_p[h].arrive_across(n)
            poly_to_sibling(h, n).start()
        for n in (4, 5, 6):
            add_product(h, n)
    for h in range(2):
        gathers_p[h].arrive(7)
        gathers_p[h].arrive_across(7)
        poly_to_sibling(h, 7).start()
    for h in range(2):
        add_product(h, 7)

    product = total[pl.ds(pl.multiple_of(core * 64, 8), TILE)]
    out[...] = (
        math.sqrt(8192) * (coef_linear * ortho[chip_row, core].astype(F32) + product)
    ).astype(BF16)

    gather_b.finish()
    for h in range(2):
        gathers_p[h].finish()
        for n in range(8):
            poly_to_sibling(h, n).wait_send()
    for n in range(8):
        from_sibling(n).wait_send()
    for t in range(6):
        for c in half_hops(t, *tasks[t]) + whole_hops(t, *tasks[t]):
            c.wait_send()
    for m in range(2):
        plane_hop(m).wait_send()
        pair_hop(m + 2).wait_send()
    for m in range(4):
        rows_gathers[m].finish()
        cols_gathers[m].finish()
        for n in range(8):
            cols_to_sibling(m, n).wait_send()


def iterate(blended):
    dma = pltpu.SemaphoreType.DMA
    return pl.pallas_call(
        kernel,
        out_shape=jax.ShapeDtypeStruct((TILE, WIDTH), BF16),
        in_specs=[pl.BlockSpec(memory_space=pltpu.VMEM)],
        out_specs=pl.BlockSpec(memory_space=pltpu.VMEM),
        scratch_shapes=[
            pltpu.VMEM((8, TILE, WIDTH), BF16),
            pltpu.VMEM((8, 2, TILE, WIDTH), BF16),
            pltpu.VMEM((2, 4, TILE, BLOCK), F32),
            pltpu.VMEM((6, 2, 40, BLOCK), F32),
            pltpu.VMEM((6, 2, PIECE, BLOCK), F32),
            pltpu.VMEM((2, TILE, BLOCK), F32),
            pltpu.VMEM((2, PIECE, BLOCK), F32),
            pltpu.VMEM((2, 4, 2, 4, PIECE, BLOCK), BF16),
            pltpu.VMEM((8, TILE, BLOCK), BF16),
            pltpu.VMEM((8, 2, 2, 160, BLOCK), BF16),
            pltpu.VMEM((160, BLOCK), F32),
            pltpu.VMEM((384, WIDTH), F32),
            pltpu.VMEM((4, 4, 8, 128), F32),
            dma((9,)), dma((9,)), dma((8,)), dma((8,)),
            dma((6, 2)), dma((6, 2)), dma((6, 2)), dma((6, 2)), dma((2,)), dma((2,)), dma((2,)), dma((2,)),
            dma((4, 9)), dma((4, 9)), dma((4, 9)), dma((4, 9)), dma((4, 8)), dma((4, 8)),
            dma((2, 12)), dma((2, 12)), dma((2, 8)), dma((2, 8)),
            dma((4, 3)), dma((4, 3)),
        ],
        compiler_params=pltpu.CompilerParams(
            collective_id=0, has_side_effects=True, vmem_limit_bytes=60 << 20
        ),
    )(blended)


def per_device(grad, momentum):
    new_momentum = momentum_decay * momentum + grad
    blended = (grad + momentum_decay * new_momentum).astype(BF16)
    return (iterate(blended), new_momentum)


def solution(mesh):
    placed = (P("row", "col"), P("row", "col"))
    return jax.shard_map(
        per_device,
        mesh=mesh,
        in_specs=placed,
        out_specs=(P("row", "col"), P("row", "col")),
        check_vma=False,
    )
```

time: 181 us -> 158 us (0.87)
  Pallas kernels: 175 us -> 152 us
    pallas_call x1, Pallas kernels: 175 us -> 152 us  [iterate(): pl.pallas_call(kernel, out_shape=jax.ShapeDtypeStruct((TILE, WIDTH), BF16...]
where the time goes in v3:
time: 158 us
  Pallas kernels  152 us (96%)
  other arithmetic  3.42 us (2%)
  local copies, waits for them, and re-layouts  1.97 us (1%)
    pallas_call x1, Pallas kernels, iterate(): pl.pallas_call(kernel, out_shape=jax.ShapeDtypeStruct((TILE, WIDTH), BF16...  152 us
    convert_element_type x1, other arithmetic, per_device(): blended = (grad + momentum_decay * new_momentum).astype(BF16)  3.42 us

profile of v3, /device:TPU:1, one launch (start us, length us, event | category | flops | bytes accessed | tf_op | source)
XLA Modules:
  0.0 158.0 jit_solution(14623851005488767633)
XLA Ops:
  0.6 3.4 %add_convert_fusion = (bf16[320,1024]{1,0:T(8,128)(2,1)}, f32[320,1024]{1,0:T(8,128)}) fusion(f32[320,1024]{1,0:T(8,128)} %param.2, f32[320,1024]{1,0:T(8,128)} %param.3), kind=kLoop, calls=%fused_computation | loop fusion | flops 1638400 | bytes 4587520 | tf_op jit(solution)/shard_map/convert_element_type | solution.py:503
  4.0 152.0 %shard_map.41 = bf16[320,1024]{1,0:T(8,128)(2,1)} custom-call(bf16[320,1024]{1,0:T(8,128)(2,1)} %get-tuple-element.2.blended), custom_call_target="tpu_custom_call" | custom-call | tf_op jit(solution)/shard_map/pallas_call | solution.py:470
  156.0 2.0 %copy.5 = bf16[320,1024]{1,0:T(8,128)(2,1)} copy(bf16[320,1024]{1,0:T(8,128)(2,1)} %shard_map.41) | data formatting | bytes 1310720

commit v4 on v3

--- a/solution.py
+++ b/solution.py
@@ -93,8 +93,8 @@
 
 def kernel(
     blended, out,
-    raw, ortho, part, hop_half, hop_whole, hop_plane, hop_pair, gram_cols, gram_rows, poly, square, total, sums,
-    b_send, b_recv, bs_send, bs_recv, half_send, half_recv, whole_send, whole_recv, plane_send, plane_recv, z_send, z_recv,
+    raw, ortho, part, hop_half, hop_whole, hop_pair, turned, turned_in, spots, gram_cols, gram_rows, poly, square, total, sums,
+    b_send, b_recv, l_send, l_recv, bs_send, bs_recv, half_send, half_recv, whole_send, whole_recv, t_send, t_recv, z_send, z_recv,
     gr_send, gr_recv, gc_send, gc_recv, gs_send, gs_recv, p_send, p_recv, ps_send, ps_recv,
     sum_send, sum_recv,
 ):
@@ -119,8 +119,8 @@
     peers = {
         "core": [sibling],
         "x": [at(x=turn(x, n)) for n in (1, 2, 3)],
+        "z": [at(z_lo=lax.rem(turn(z, n), 2), z_hi=lax.div(turn(z, n), 2)) for n in (1, 2, 3)],
         "y": [at(y=turn(y, n)) for n in (1, 2, 3)],
-        "z": [at(z_lo=lax.rem(turn(z, n), 2), z_hi=lax.div(turn(z, n), 2)) for n in (1, 2, 3)],
     }
     everyone = [d for group in peers.values() for d in group]
 
@@ -129,19 +129,33 @@
         pl.semaphore_signal(barrier, inc=1, device_id=d, device_id_type=MESH)
     pl.semaphore_wait(barrier, len(everyone))
 
-    gather_b = Gather(
-        blended,
-        lambda p, b: raw.at[b * 4 + p],
-        lambda p, b, first, rows: raw.at[b * 4 + p, pl.ds(first, rows)],
-        TILE, 160, x, z_lo, x_right, x_left, lo_pair, b_send, b_recv,
-    )
-    gather_b.start()
+    lo, hi, opp = turn(x, 3), turn(x, 1), turn(x, 2)
+    high = lax.div(x, 2)
+    to_opp = high * z_lo + (1 - high) * (1 - z_lo)
+    from_opp = (1 - high) * z_lo + high * (1 - z_lo)
+
+    def b_copy(n, b, device, first=0, rows=TILE):
+        place = raw.at[b * 4 + x, pl.ds(first, rows)]
+        return pltpu.make_async_remote_copy(
+            place, place, b_send.at[n], b_recv.at[n], device_id=device, device_id_type=MESH
+        )
+
+    across = [b_copy(0, z_lo, lo_pair, 0, 128), b_copy(1, z_lo, lo_pair, 128, 192)]
+    own_left = b_copy(2, z_lo, x_left)
+    other_right = [b_copy(3, 1 - z_lo, x_right, 0, 128), b_copy(4, 1 - z_lo, x_right, 128, 192)]
+    first_opp = b_copy(5, to_opp, at(x=opp))
+    order = [
+        (x, z_lo), (x, 1 - z_lo), (hi, z_lo), (lo, 1 - z_lo), (opp, from_opp),
+        (hi, 1 - z_lo), (lo, z_lo), (opp, 1 - from_opp),
+    ]
+    raw[z_lo * 4 + x] = blended[...]
+    across[0].start()
 
     mine = jnp.zeros((8, 128), F32)
     for k in range(8):
         wide = blended[:, k * 128 : (k + 1) * 128].astype(F32).reshape(TILE // 8, 8, 128)
         mine = mine + jnp.sum(wide * wide, axis=0)
-    for stage, (place, size) in enumerate(((core, 2), (x, 4), (y, 4), (z, 4))):
+    for stage, (place, size) in enumerate(((core, 2), (x, 4), (z, 4), (y, 4))):
         group = list(peers.values())[stage]
         sums[stage, place] = mine
         copies = [
@@ -158,6 +172,11 @@
         mine = sums[stage, 0]
         for n in range(1, size):
             mine = mine + sums[stage, n]
+        if stage == 1:
+            own_left.start()
+            pl.when(high == 1)(first_opp.start)
+        elif stage == 2:
+            across[1].start()
     squares_total = jnp.sum(mine, keepdims=True)
     norm_scale = target_rms * math.sqrt(5120) / (jnp.sqrt(squares_total) + norm_epsilon)
 
@@ -205,25 +224,14 @@
             for k, (near, d) in enumerate(((turn(y, 1), y_right), (turn(y, 3), y_left)))
         ]
 
-    order = gather_b.order
-    lo, hi, opp = turn(x, 3), turn(x, 1), turn(x, 2)
     places = (x, lo, hi, opp)
 
-    def plane_hop(m):
-        return pltpu.make_async_remote_copy(
-            part.at[1 - z_hi, places[m]], hop_plane.at[m],
-            plane_send.at[m], plane_recv.at[m], device_id=hi_pair, device_id_type=MESH,
-        )
-
-    def pair_hop(m):
-        return pltpu.make_async_remote_copy(
-            part.at[1 - z_hi, places[m], mine_rows], hop_pair.at[m - 2],
-            z_send.at[m - 2], z_recv.at[m - 2], device_id=hi_pair, device_id_type=MESH,
-        )
-
-    tasks = ((x, z_hi), (lo, z_hi), (hi, z_lo), (hi, 1 - z_lo), (opp, z_lo), (opp, 1 - z_lo))
+    planes = (None, 1 - z_lo, z_lo, from_opp)
+
+    tasks = ((x, z_lo), (x, 1 - z_lo), (lo, 1 - z_lo), (hi, z_lo), (opp, from_opp))
 
     def reduce_1(t):
+        partial(*tasks[t])
         for c in half_hops(t, *tasks[t]):
             c.start()
 
@@ -242,32 +250,83 @@
             c.wait_recv()
         part[b, p, mine_rows] = part[b, p, mine_rows] + (hop_whole[t, 0] + hop_whole[t, 1])
 
-    def add_planes(m):
-        plane_hop(m).wait_recv()
-        part[z_hi, places[m]] = part[z_hi, places[m]] + hop_plane[m]
-        reduce_1(m)
-
-    def finish_tile(m):
+    def pair_hop(m):
+        b = 1 - z_hi if m == 0 else planes[m]
+        return pltpu.make_async_remote_copy(
+            part.at[b, places[m], mine_rows], hop_pair.at[m],
+            z_send.at[m], z_recv.at[m], device_id=hi_pair, device_id_type=MESH,
+        )
+
+    def reduce_4(m):
+        if m == 0:
+            pair_hop(0).start()
+        else:
+            pl.when(planes[m] != z_hi)(lambda: pair_hop(m).start())
+
+    def keep(m, tile):
         p = places[m]
-        tile = part[z_hi, p, mine_rows]
-        if m >= 2:
-            pair_hop(m).wait_recv()
-            tile = tile + hop_pair[m - 2]
-        tile = tile.astype(BF16)
         gram_cols[z_hi, p, core, y] = tile
         gram_rows[chip_row, pl.ds(pl.multiple_of(p * PIECE, 16), PIECE)] = tile
+
+    def summed(m):
+        pair_hop(m).wait_recv()
+        return part[z_hi, places[m], mine_rows] + hop_pair[m]
+
+    def turned_pieces(m):
+        away = (0, 2, 1, 3)[m]
+        return [
+            pltpu.make_async_remote_copy(
+                turned.at[m - 1, a * 4 + k], turned_in.at[away - 1, core * 4 + y],
+                t_send.at[m - 1], t_recv.at[away - 1],
+                device_id=((z_hi * 4 + places[m]) * 2 + a, k * 2 + z_lo), device_id_type=MESH,
+            )
+            for a in range(2) for k in range(4)
+        ]
+
+    def all_turned(m):
+        return pltpu.make_async_remote_copy(
+            turned.at[m - 1], turned_in.at[m - 1],
+            t_send.at[m - 1], t_recv.at[m - 1], device_id=sibling, device_id_type=MESH,
+        )
+
+    def reduce_5(m):
+        @pl.when(planes[m] == z_hi)
+        def _():
+            tile = summed(m)
+            keep(m, tile.astype(BF16))
+            tall = jnp.concatenate([tile, jnp.zeros((128 - PIECE, BLOCK), F32)], axis=0).T
+            turned[m - 1] = tall.astype(BF16).reshape(8, PIECE, 128)
+            for c in turned_pieces(m):
+                c.start()
+
+    def finish_tile(m):
+        if m == 0:
+            keep(0, summed(0).astype(BF16))
+            return
+
+        @pl.when(planes[m] != z_hi)
+        def _():
+            all_turned(m).wait_recv()
+            wide = jnp.concatenate([turned_in[m - 1, k] for k in range(8)], axis=1)
+            keep(m, jnp.dot(wide, spots[...], preferred_element_type=F32).astype(BF16))
 
     def from_sibling(n):
         p, b = order[n]
         return to_sibling(n, ortho.at[b * 4 + p, core], bs_send, bs_recv)
 
+    def later(k):
+        p, b = order[2 + k // 4]
+        place = ortho.at[b * 4 + p, core, pl.ds(k % 4 * 80, 80)]
+        return pltpu.make_async_remote_copy(
+            place, place, l_send.at[k], l_recv.at[k], device_id=lo_pair, device_id_type=MESH
+        )
+
     def process(n):
         p, b = order[n]
-        scale(blended if n == 0 else raw.at[b * 4 + p], b * 4 + p)
+        scale(raw.at[b * 4 + p], b * 4 + p)
         from_sibling(n).start()
         if n == 0:
             from_sibling(0).wait_recv()
-        partial(p, b)
 
     def gather_rows(m):
         def place(p, b, first, rows):
@@ -309,58 +368,73 @@
             cols_to_sibling(m, n).start()
             rows_gathers[m].arrive(n)
 
+    spot = lax.broadcasted_iota(jnp.int32, (WIDTH, BLOCK), 0)
+    column = lax.broadcasted_iota(jnp.int32, (WIDTH, BLOCK), 1)
+    lane = spot % 128
+    spots[...] = jnp.where((lane < PIECE) & (column == spot // 128 * PIECE + lane), 1.0, 0.0).astype(BF16)
+
+    across[0].wait_recv()
+    other_right[0].start()
     process(0)
-    for n in (1, 2, 3):
-        gather_b.arrive(n)
+    reduce_1(0)
+    across[1].wait_recv()
+    other_right[1].start()
+    pl.when(high == 0)(first_opp.start)
     process(1)
-    plane_hop(0).start()
+    reduce_1(1)
+    reduce_2(0)
+    own_left.wait_recv()
+    process(2)
+    reduce_1(3)
+    reduce_2(1)
+    for k in range(4):
+        later(k).start()
+    reduce_3(0)
+    reduce_2(3)
+    reduce_3(1)
+    reduce_4(0)
+    for c in other_right:
+        c.wait_recv()
     process(3)
     reduce_1(2)
-    process(2)
+    reduce_3(3)
+    reduce_4(2)
+    later(4).start()
+    later(5).start()
+    first_opp.wait_recv()
+    process(4)
+    reduce_1(4)
+    spread(0, 0)
     reduce_2(2)
-    gather_b.arrive(4)
-    gather_b.arrive(5)
-    process(4)
-    plane_hop(1).start()
-    process(5)
-    reduce_1(3)
+    reduce_5(2)
+    reduce_2(4)
+    later(6).start()
+    spread(0, 1)
+    later(7).start()
     reduce_3(2)
-    add_planes(0)
-    reduce_2(3)
-    gather_b.arrive(6)
-    process(6)
-    reduce_1(4)
-    reduce_2(0)
-    reduce_3(3)
-    pair_hop(2).start()
-    gather_b.arrive(7)
-    process(7)
-    reduce_1(5)
-    reduce_2(4)
-    reduce_3(0)
-    spread(0, 0)
-    reduce_2(5)
+    reduce_4(1)
+    reduce_3(4)
+    reduce_4(3)
+    spread(0, 2)
+    reduce_5(1)
+    spread(1, 0)
+    reduce_5(3)
+    later(8).start()
     spread(2, 0)
-    add_planes(1)
-    reduce_3(4)
-    spread(0, 1)
-    reduce_3(5)
-    pair_hop(3).start()
+    spread(0, 3)
+    spread(1, 1)
+    later(9).start()
+    spread(3, 0)
     spread(2, 1)
-    reduce_2(1)
-    spread(0, 2)
+    spread(1, 2)
+    later(10).start()
+    spread(3, 1)
+    later(11).start()
     spread(2, 2)
-    spread(3, 0)
-    reduce_3(1)
-    spread(1, 0)
-    spread(0, 3)
+    spread(3, 2)
+    spread(1, 3)
     spread(2, 3)
-    spread(3, 1)
-    spread(1, 1)
-    spread(3, 2)
-    spread(1, 2)
     spread(3, 3)
-    spread(1, 3)
     for m in range(4):
         for n in range(8):
             cols_to_sibling(m, n).wait_recv()
@@ -398,6 +472,10 @@
         gathers_p[h].start()
         poly_to_sibling(h, 0).start()
 
+    for k in range(12):
+        later(k).wait_recv()
+        if k % 4 == 3:
+            from_sibling(5 + k // 4).start()
     for n in range(1, 8):
         from_sibling(n).wait_recv()
 
@@ -445,19 +523,21 @@
         math.sqrt(8192) * (coef_linear * ortho[chip_row, core].astype(F32) + product)
     ).astype(BF16)
 
-    gather_b.finish()
+    for c in across + other_right + [own_left, first_opp] + [later(k) for k in range(12)]:
+        c.wait_send()
     for h in range(2):
         gathers_p[h].finish()
         for n in range(8):
             poly_to_sibling(h, n).wait_send()
     for n in range(8):
         from_sibling(n).wait_send()
-    for t in range(6):
+    for t in range(5):
         for c in half_hops(t, *tasks[t]) + whole_hops(t, *tasks[t]):
             c.wait_send()
-    for m in range(2):
-        plane_hop(m).wait_send()
-        pair_hop(m + 2).wait_send()
+    pair_hop(0).wait_send()
+    for m in (1, 2, 3):
+        pl.when(planes[m] != z_hi)(lambda m=m: pair_hop(m).wait_send())
+        pl.when(planes[m] == z_hi)(lambda m=m: all_turned(m).wait_send())
     for m in range(4):
         rows_gathers[m].finish()
         cols_gathers[m].finish()
@@ -476,18 +556,20 @@
             pltpu.VMEM((8, TILE, WIDTH), BF16),
             pltpu.VMEM((8, 2, TILE, WIDTH), BF16),
             pltpu.VMEM((2, 4, TILE, BLOCK), F32),
-            pltpu.VMEM((6, 2, 40, BLOCK), F32),
-            pltpu.VMEM((6, 2, PIECE, BLOCK), F32),
-            pltpu.VMEM((2, TILE, BLOCK), F32),
-            pltpu.VMEM((2, PIECE, BLOCK), F32),
+            pltpu.VMEM((5, 2, 40, BLOCK), F32),
+            pltpu.VMEM((5, 2, PIECE, BLOCK), F32),
+            pltpu.VMEM((4, PIECE, BLOCK), F32),
+            pltpu.VMEM((3, 8, PIECE, 128), BF16),
+            pltpu.VMEM((3, 8, PIECE, 128), BF16),
+            pltpu.VMEM((WIDTH, BLOCK), BF16),
             pltpu.VMEM((2, 4, 2, 4, PIECE, BLOCK), BF16),
             pltpu.VMEM((8, TILE, BLOCK), BF16),
             pltpu.VMEM((8, 2, 2, 160, BLOCK), BF16),
             pltpu.VMEM((160, BLOCK), F32),
             pltpu.VMEM((384, WIDTH), F32),
             pltpu.VMEM((4, 4, 8, 128), F32),
-            dma((9,)), dma((9,)), dma((8,)), dma((8,)),
-            dma((6, 2)), dma((6, 2)), dma((6, 2)), dma((6, 2)), dma((2,)), dma((2,)), dma((2,)), dma((2,)),
+            dma((6,)), dma((6,)), dma((12,)), dma((12,)), dma((8,)), dma((8,)),
+            dma((5, 2)), dma((5, 2)), dma((5, 2)), dma((5, 2)), dma((3,)), dma((3,)), dma((4,)), dma((4,)),
             dma((4, 9)), dma((4, 9)), dma((4, 9)), dma((4, 9)), dma((4, 8)), dma((4, 8)),
             dma((2, 12)), dma((2, 12)), dma((2, 8)), dma((2, 8)),
             dma((4, 3)), dma((4, 3)),

time: 158 us -> 152 us (0.962)
  Pallas kernels: 152 us -> 146 us
    pallas_call x1, Pallas kernels: 152 us -> 146 us  [iterate(): pl.pallas_call(kernel, out_shape=jax.ShapeDtypeStruct((TILE, WIDTH), BF16...]
where the time goes in v4:
time: 152 us
  Pallas kernels  146 us (96%)
  other arithmetic  3.42 us (2%)
  local copies, waits for them, and re-layouts  1.97 us (1%)
    pallas_call x1, Pallas kernels, iterate(): pl.pallas_call(kernel, out_shape=jax.ShapeDtypeStruct((TILE, WIDTH), BF16...  146 us
    convert_element_type x1, other arithmetic, per_device(): blended = (grad + momentum_decay * new_momentum).astype(BF16)  3.42 us

profile of v4, /device:TPU:1, one launch (start us, length us, event | category | flops | bytes accessed | tf_op | source)
XLA Modules:
  0.0 152.0 jit_solution(10714069598779044018)
XLA Ops:
  0.6 3.4 %add_convert_fusion = (bf16[320,1024]{1,0:T(8,128)(2,1)}, f32[320,1024]{1,0:T(8,128)}) fusion(f32[320,1024]{1,0:T(8,128)} %param.2, f32[320,1024]{1,0:T(8,128)} %param.3), kind=kLoop, calls=%fused_computation | loop fusion | flops 1638400 | bytes 4587520 | tf_op jit(solution)/shard_map/convert_element_type | solution.py:585
  4.0 145.9 %shard_map.41 = bf16[320,1024]{1,0:T(8,128)(2,1)} custom-call(bf16[320,1024]{1,0:T(8,128)(2,1)} %get-tuple-element.2.blended), custom_call_target="tpu_custom_call" | custom-call | tf_op jit(solution)/shard_map/pallas_call | solution.py:550
  150.0 2.0 %copy.5 = bf16[320,1024]{1,0:T(8,128)(2,1)} copy(bf16[320,1024]{1,0:T(8,128)(2,1)} %shard_map.41) | data formatting | bytes 1310720

commit v5 on v4

--- a/solution.py
+++ b/solution.py
@@ -315,6 +315,11 @@
         return to_sibling(n, ortho.at[b * 4 + p, core], bs_send, bs_recv)
 
     def later(k):
+        if k == 8:
+            place = ortho.at[(1 - to_opp) * 4 + x, core]
+            return pltpu.make_async_remote_copy(
+                place, place, l_send.at[8], l_recv.at[8], device_id=at(x=opp), device_id_type=MESH
+            )
         p, b = order[2 + k // 4]
         place = ortho.at[b * 4 + p, core, pl.ds(k % 4 * 80, 80)]
         return pltpu.make_async_remote_copy(
@@ -419,17 +424,13 @@
     reduce_5(1)
     spread(1, 0)
     reduce_5(3)
-    later(8).start()
     spread(2, 0)
     spread(0, 3)
     spread(1, 1)
-    later(9).start()
     spread(3, 0)
     spread(2, 1)
     spread(1, 2)
-    later(10).start()
     spread(3, 1)
-    later(11).start()
     spread(2, 2)
     spread(3, 2)
     spread(1, 3)
@@ -467,63 +468,77 @@
         p, b = gathers_p[h].order[n]
         return to_sibling(n, poly.at[p * 2 + b, h, core], ps_send.at[h], ps_recv.at[h])
 
+    later(8).start()
     for h in range(2):
         half_of_poly(h)
         gathers_p[h].start()
         poly_to_sibling(h, 0).start()
 
-    for k in range(12):
-        later(k).wait_recv()
-        if k % 4 == 3:
-            from_sibling(5 + k // 4).start()
-    for n in range(1, 8):
-        from_sibling(n).wait_recv()
-
     lanes = pl.ds(pl.multiple_of(core * 256, 128), 384)
     total[...] = jnp.zeros_like(total)
 
-    def add_product(h, n):
-        poly_to_sibling(h, n).wait_recv()
-        p, b = gathers_p[h].order[n]
+    def add_product(n, columns):
+        p, b = gathers_p[0].order[n]
         first = pl.multiple_of(p * PIECE, 16)
-        left = poly[p * 2 + b, h, :, :, lanes].reshape(TILE, 384)
-        right = jnp.concatenate(
-            [ortho[b * 4 + 2 * h + k, a, pl.ds(first, PIECE)] for a in range(2) for k in range(2)], axis=0
-        )
+        left = [
+            poly[p * 2 + b, lax.div(q, 2), a, pl.ds(pl.multiple_of(lax.rem(q, 2) * PIECE, 16), PIECE), lanes]
+            for q in columns for a in range(2)
+        ]
+        right = [ortho[b * 4 + q, a, pl.ds(first, PIECE)] for q in columns for a in range(2)]
         total[...] += lax.dot_general(
-            left, right, (((0,), (0,)), ((), ())), preferred_element_type=F32
-        )
+            jnp.concatenate(left, axis=0), jnp.concatenate(right, axis=0),
+            (((0,), (0,)), ((), ())), preferred_element_type=F32,
+        )
+
+    near, far = (x, hi), (lo, opp)
 
     for h in range(2):
         for n in (1, 2, 3):
             gathers_p[h].arrive(n)
             poly_to_sibling(h, n).start()
-    for h in range(2):
-        for n in range(4):
-            add_product(h, n)
+    for k in range(8):
+        later(k).wait_recv()
+        if k % 4 == 3:
+            from_sibling(5 + k // 4).start()
+    for n in range(1, 7):
+        from_sibling(n).wait_recv()
+    for n in range(4):
+        for h in range(2):
+            poly_to_sibling(h, n).wait_recv()
+        add_product(n, near)
     for h in range(2):
         gathers_p[h].arrive(6)
         poly_to_sibling(h, 6).start()
         for n in (4, 5):
             gathers_p[h].arrive(n)
+    later(8).wait_recv()
+    from_sibling(7).start()
+    for h in range(2):
         for n in (4, 5):
             gathers_p[h].arrive_across(n)
             poly_to_sibling(h, n).start()
-        for n in (4, 5, 6):
-            add_product(h, n)
+    for n in (4, 5, 6):
+        for h in range(2):
+            poly_to_sibling(h, n).wait_recv()
+        add_product(n, near)
+    from_sibling(7).wait_recv()
+    for n in range(7):
+        add_product(n, far)
     for h in range(2):
         gathers_p[h].arrive(7)
         gathers_p[h].arrive_across(7)
         poly_to_sibling(h, 7).start()
     for h in range(2):
-        add_product(h, 7)
+        poly_to_sibling(h, 7).wait_recv()
+    add_product(7, near)
+    add_product(7, far)
 
     product = total[pl.ds(pl.multiple_of(core * 64, 8), TILE)]
     out[...] = (
         math.sqrt(8192) * (coef_linear * ortho[chip_row, core].astype(F32) + product)
     ).astype(BF16)
 
-    for c in across + other_right + [own_left, first_opp] + [later(k) for k in range(12)]:
+    for c in across + other_right + [own_left, first_opp] + [later(k) for k in range(9)]:
         c.wait_send()
     for h in range(2):
         gathers_p[h].finish()
@@ -568,7 +583,7 @@
             pltpu.VMEM((160, BLOCK), F32),
             pltpu.VMEM((384, WIDTH), F32),
             pltpu.VMEM((4, 4, 8, 128), F32),
-            dma((6,)), dma((6,)), dma((12,)), dma((12,)), dma((8,)), dma((8,)),
+            dma((6,)), dma((6,)), dma((9,)), dma((9,)), dma((8,)), dma((8,)),
             dma((5, 2)), dma((5, 2)), dma((5, 2)), dma((5, 2)), dma((3,)), dma((3,)), dma((4,)), dma((4,)),
             dma((4, 9)), dma((4, 9)), dma((4, 9)), dma((4, 9)), dma((4, 8)), dma((4, 8)),
             dma((2, 12)), dma((2, 12)), dma((2, 8)), dma((2, 8)),

time: 152 us -> 150 us (0.987)
  Pallas kernels: 146 us -> 143 us
    pallas_call x1, Pallas kernels: 146 us -> 143 us  [iterate(): pl.pallas_call(kernel, out_shape=jax.ShapeDtypeStruct((TILE, WIDTH), BF16...]
where the time goes in v5:
time: 150 us; the launch traced here: 149 us
  Pallas kernels  143 us (95%)
  other arithmetic  3.42 us (2%)
  local copies, waits for them, and re-layouts  1.97 us (1%)
    pallas_call x1, Pallas kernels, iterate(): pl.pallas_call(kernel, out_shape=jax.ShapeDtypeStruct((TILE, WIDTH), BF16...  143 us
    convert_element_type x1, other arithmetic, per_device(): blended = (grad + momentum_decay * new_momentum).astype(BF16)  3.42 us

profile of v5, /device:TPU:1, one launch (start us, length us, event | category | flops | bytes accessed | tf_op | source)
XLA Modules:
  0.0 148.6 jit_solution(5280364227035661432)
XLA Ops:
  0.6 3.4 %add_convert_fusion = (bf16[320,1024]{1,0:T(8,128)(2,1)}, f32[320,1024]{1,0:T(8,128)}) fusion(f32[320,1024]{1,0:T(8,128)} %param.2, f32[320,1024]{1,0:T(8,128)} %param.3), kind=kLoop, calls=%fused_computation | loop fusion | flops 1638400 | bytes 4587520 | tf_op jit(solution)/shard_map/convert_element_type | solution.py:600
  4.0 142.5 %shard_map.41 = bf16[320,1024]{1,0:T(8,128)(2,1)} custom-call(bf16[320,1024]{1,0:T(8,128)(2,1)} %get-tuple-element.2.blended), custom_call_target="tpu_custom_call" | custom-call | tf_op jit(solution)/shard_map/pallas_call | solution.py:565
  146.6 2.0 %copy.5 = bf16[320,1024]{1,0:T(8,128)(2,1)} copy(bf16[320,1024]{1,0:T(8,128)(2,1)} %shard_map.41) | data formatting | bytes 1310720

commit v6 on v5

--- a/solution.py
+++ b/solution.py
@@ -320,10 +320,11 @@
             return pltpu.make_async_remote_copy(
                 place, place, l_send.at[8], l_recv.at[8], device_id=at(x=opp), device_id_type=MESH
             )
-        p, b = order[2 + k // 4]
+        p, b = (x, 1 - z_lo if k < 4 else z_lo)
         place = ortho.at[b * 4 + p, core, pl.ds(k % 4 * 80, 80)]
         return pltpu.make_async_remote_copy(
-            place, place, l_send.at[k], l_recv.at[k], device_id=lo_pair, device_id_type=MESH
+            place, place, l_send.at[k], l_recv.at[k],
+                device_id=x_left if k < 4 else x_right, device_id_type=MESH
         )
 
     def process(n):
@@ -392,8 +393,6 @@
     process(2)
     reduce_1(3)
     reduce_2(1)
-    for k in range(4):
-        later(k).start()
     reduce_3(0)
     reduce_2(3)
     reduce_3(1)
@@ -404,7 +403,9 @@
     reduce_1(2)
     reduce_3(3)
     reduce_4(2)
+    later(0).start()
     later(4).start()
+    later(1).start()
     later(5).start()
     first_opp.wait_recv()
     process(4)
@@ -413,8 +414,10 @@
     reduce_2(2)
     reduce_5(2)
     reduce_2(4)
+    later(2).start()
     later(6).start()
     spread(0, 1)
+    later(3).start()
     later(7).start()
     reduce_3(2)
     reduce_4(1)

time: 150 us -> 145 us (0.967)
  Pallas kernels: 143 us -> 138 us
    pallas_call x1, Pallas kernels: 143 us -> 138 us  [iterate(): pl.pallas_call(kernel, out_shape=jax.ShapeDtypeStruct((TILE, WIDTH), BF16...]
where the time goes in v6:
time: 145 us; the launch traced here: 144 us
  Pallas kernels  138 us (95%)
  other arithmetic  3.42 us (2%)
  local copies, waits for them, and re-layouts  1.97 us (1%)
    pallas_call x1, Pallas kernels, iterate(): pl.pallas_call(kernel, out_shape=jax.ShapeDtypeStruct((TILE, WIDTH), BF16...  138 us
    convert_element_type x1, other arithmetic, per_device(): blended = (grad + momentum_decay * new_momentum).astype(BF16)  3.42 us

profile of v6, /device:TPU:1, one launch (start us, length us, event | category | flops | bytes accessed | tf_op | source)
XLA Modules:
  0.0 143.7 jit_solution(13353504709975607624)
XLA Ops:
  0.6 3.4 %add_convert_fusion = (bf16[320,1024]{1,0:T(8,128)(2,1)}, f32[320,1024]{1,0:T(8,128)}) fusion(f32[320,1024]{1,0:T(8,128)} %param.2, f32[320,1024]{1,0:T(8,128)} %param.3), kind=kLoop, calls=%fused_computation | loop fusion | flops 1638400 | bytes 4587520 | tf_op jit(solution)/shard_map/convert_element_type | solution.py:603
  4.0 137.7 %shard_map.41 = bf16[320,1024]{1,0:T(8,128)(2,1)} custom-call(bf16[320,1024]{1,0:T(8,128)(2,1)} %get-tuple-element.2.blended), custom_call_target="tpu_custom_call" | custom-call | tf_op jit(solution)/shard_map/pallas_call | solution.py:568
  141.7 2.0 %copy.5 = bf16[320,1024]{1,0:T(8,128)(2,1)} copy(bf16[320,1024]{1,0:T(8,128)(2,1)} %shard_map.41) | data formatting | bytes 1310720

commit v7 on v6

--- a/solution.py
+++ b/solution.py
@@ -177,6 +177,8 @@
             pl.when(high == 1)(first_opp.start)
         elif stage == 2:
             across[1].start()
+            across[0].wait_recv()
+            other_right[0].start()
     squares_total = jnp.sum(mine, keepdims=True)
     norm_scale = target_rms * math.sqrt(5120) / (jnp.sqrt(squares_total) + norm_epsilon)
 
@@ -379,8 +381,6 @@
     lane = spot % 128
     spots[...] = jnp.where((lane < PIECE) & (column == spot // 128 * PIECE + lane), 1.0, 0.0).astype(BF16)
 
-    across[0].wait_recv()
-    other_right[0].start()
     process(0)
     reduce_1(0)
     across[1].wait_recv()
@@ -401,10 +401,10 @@
         c.wait_recv()
     process(3)
     reduce_1(2)
+    later(0).start()
+    later(4).start()
     reduce_3(3)
     reduce_4(2)
-    later(0).start()
-    later(4).start()
     later(1).start()
     later(5).start()
     first_opp.wait_recv()

time: 145 us -> 144 us (level)
  no operation moved by 1% of the time
where the time goes in v7:
time: 144 us; the launch traced here: 143 us
  Pallas kernels  137 us (95%)
  other arithmetic  3.42 us (2%)
  local copies, waits for them, and re-layouts  1.97 us (1%)
    pallas_call x1, Pallas kernels, iterate(): pl.pallas_call(kernel, out_shape=jax.ShapeDtypeStruct((TILE, WIDTH), BF16...  137 us
    convert_element_type x1, other arithmetic, per_device(): blended = (grad + momentum_decay * new_momentum).astype(BF16)  3.42 us

profile of v7, /device:TPU:1, one launch (start us, length us, event | category | flops | bytes accessed | tf_op | source)
XLA Modules:
  0.0 142.6 jit_solution(395247746291645624)
XLA Ops:
  0.6 3.4 %add_convert_fusion = (bf16[320,1024]{1,0:T(8,128)(2,1)}, f32[320,1024]{1,0:T(8,128)}) fusion(f32[320,1024]{1,0:T(8,128)} %param.2, f32[320,1024]{1,0:T(8,128)} %param.3), kind=kLoop, calls=%fused_computation | loop fusion | flops 1638400 | bytes 4587520 | tf_op jit(solution)/shard_map/convert_element_type | solution.py:603
  4.0 136.6 %shard_map.41 = bf16[320,1024]{1,0:T(8,128)(2,1)} custom-call(bf16[320,1024]{1,0:T(8,128)(2,1)} %get-tuple-element.2.blended), custom_call_target="tpu_custom_call" | custom-call | tf_op jit(solution)/shard_map/pallas_call | solution.py:568
  140.6 2.0 %copy.5 = bf16[320,1024]{1,0:T(8,128)(2,1)} copy(bf16[320,1024]{1,0:T(8,128)(2,1)} %shard_map.41) | data formatting | bytes 1310720

commit v8 on v7

--- a/solution.py
+++ b/solution.py
@@ -439,6 +439,7 @@
     spread(1, 3)
     spread(2, 3)
     spread(3, 3)
+    later(8).start()
     for m in range(4):
         for n in range(8):
             cols_to_sibling(m, n).wait_recv()
@@ -471,7 +472,6 @@
         p, b = gathers_p[h].order[n]
         return to_sibling(n, poly.at[p * 2 + b, h, core], ps_send.at[h], ps_recv.at[h])
 
-    later(8).start()
     for h in range(2):
         half_of_poly(h)
         gathers_p[h].start()

time: 144 us -> 144 us (level)
  no operation moved by 1% of the time
where the time goes in v8:
time: 144 us; the launch traced here: 143 us
  Pallas kernels  137 us (95%)
  other arithmetic  3.42 us (2%)
  local copies, waits for them, and re-layouts  1.97 us (1%)
    pallas_call x1, Pallas kernels, iterate(): pl.pallas_call(kernel, out_shape=jax.ShapeDtypeStruct((TILE, WIDTH), BF16...  137 us
    convert_element_type x1, other arithmetic, per_device(): blended = (grad + momentum_decay * new_momentum).astype(BF16)  3.42 us

profile of v8, /device:TPU:1, one launch (start us, length us, event | category | flops | bytes accessed | tf_op | source)
XLA Modules:
  0.0 142.6 jit_solution(915887924060845999)
XLA Ops:
  0.6 3.4 %add_convert_fusion = (bf16[320,1024]{1,0:T(8,128)(2,1)}, f32[320,1024]{1,0:T(8,128)}) fusion(f32[320,1024]{1,0:T(8,128)} %param.2, f32[320,1024]{1,0:T(8,128)} %param.3), kind=kLoop, calls=%fused_computation | loop fusion | flops 1638400 | bytes 4587520 | tf_op jit(solution)/shard_map/convert_element_type | solution.py:603
  4.0 136.6 %shard_map.41 = bf16[320,1024]{1,0:T(8,128)(2,1)} custom-call(bf16[320,1024]{1,0:T(8,128)(2,1)} %get-tuple-element.2.blended), custom_call_target="tpu_custom_call" | custom-call | tf_op jit(solution)/shard_map/pallas_call | solution.py:568
  140.6 2.0 %copy.5 = bf16[320,1024]{1,0:T(8,128)(2,1)} copy(bf16[320,1024]{1,0:T(8,128)(2,1)} %shard_map.41) | data formatting | bytes 1310720
